TPU v7x, 32 devices: a whole 2x2x4 slice. The times are simulated.
32 devices in a mesh: row: 4 (over y, x), col: 8 (over z, core).
Axes of the slice: x: 2, y: 2, z: 4, core: 2. Of those that a mesh axis runs over, the one named last changes fastest.
Arguments:
- iterate: float32 [128, 1024], P('row', 'col'), may hold values from 0 to 2
- gradient: float32 [128, 1024], P('row', 'col'), may hold values from -6 to 6
- dual_coeffs: float32 [8, 7, 128, 1024], P(None, None, 'row', 'col'), may hold values from -3 to 3
- weights: float32 [8, 7], replicated, may hold values from 0.2 to 2
Outputs:
- new_image: float32 [128, 1024], P('row', 'col')
- new_duals: float32 [8, 7, 128, 1024], P(None, None, 'row', 'col')
All inputs are finite; a program needn't handle non-finite values.
Results may differ from a plain program's by a relative error of at most 0.0001.
Values sent between devices are 32-bit elements; how exact they have to be, the bound alone decides.
A program may use at most 64 MiB of HBM per device.

v0:
```python
import math

import jax
import jax.numpy as jnp
import numpy as np
from jax import lax
from jax.sharding import PartitionSpec as P

BASES = 8
LEVELS = 2


primal_step = 0.5
daubechies_table = [
    [0.7071067811865476, 0.7071067811865476],
    [0.48296291314469025, 0.836516303737469, 0.22414386804185735, -0.12940952255092145],
    [
        0.3326705529509569,
        0.8068915093133388,
        0.4598775021193313,
        -0.13501102001039084,
        -0.08544127388224149,
        0.035226291882100656,
    ],
    [
        0.23037781330885523,
        0.7148465705525415,
        0.6308807679295904,
        -0.02798376941698385,
        -0.18703481171888114,
        0.030841381835986965,
        0.032883011666982945,
        -0.010597401784997278,
    ],
    [
        0.160102397974125,
        0.6038292697974729,
        0.7243085284385744,
        0.13842814590110342,
        -0.24229488706619015,
        -0.03224486958502952,
        0.07757149384006515,
        -0.006241490213011705,
        -0.012580751999015526,
        0.003335725285001549,
    ],
    [
        0.11154074335008017,
        0.4946238903983854,
        0.7511339080215775,
        0.3152503517092432,
        -0.22626469396516913,
        -0.12976686756709563,
        0.09750160558707936,
        0.02752286553001629,
        -0.031582039318031156,
        0.0005538422009938016,
        0.004777257511010651,
        -0.00107730108499558,
    ],
    [
        0.07785205408506236,
        0.39653931948230575,
        0.7291320908465551,
        0.4697822874053586,
        -0.14390600392910627,
        -0.22403618499416572,
        0.07130921926705004,
        0.0806126091510659,
        -0.03802993693503463,
        -0.01657454163101562,
        0.012550998556013784,
        0.00042957797300470274,
        -0.0018016407039998328,
        0.0003537138000010399,
    ],
    [
        0.05441584224308161,
        0.3128715909144659,
        0.6756307362980128,
        0.5853546836548691,
        -0.015829105256023893,
        -0.2840155429624281,
        0.00047248457399797254,
        0.128747426620186,
        -0.01736930100202211,
        -0.04408825393106472,
        0.013981027917015516,
        0.008746094047015655,
        -0.00487035299301066,
        -0.0003917403729959771,
        0.0006754494059985568,
        -0.00011747678400228192,
    ],
]


def with_halo(block, sides, width):
    for axis, dim in sides:
        count = lax.axis_size(axis)
        forward = [(i, i + 1) for i in range(count - 1)]
        forward.append((count - 1, 0))
        backward = [(target, source) for source, target in forward]
        low = lax.ppermute(
            lax.slice_in_dim(block, block.shape[dim] - width, None, axis=dim), axis, forward
        )
        high = lax.ppermute(lax.slice_in_dim(block, 0, width, axis=dim), axis, backward)
        block = jnp.concatenate([low, block, high], axis=dim)
    return block


def tap_tables():
    low_table = np.zeros((BASES, 16))
    high_table = np.zeros((BASES, 16))
    for basis_index in range(BASES):
        taps = np.array(daubechies_table[basis_index])
        low_taps = taps * math.sqrt(2.0) / np.sum(taps) / math.sqrt(2.0)
        length = len(low_taps)
        half_len = length // 2
        for position in range(length):
            low_table[basis_index, position - half_len + 8] = low_taps[position]
            high_table[basis_index, position - half_len + 8] = (-1.0) ** position * low_taps[
                length - 1 - position
            ]
    return (jnp.asarray(low_table, jnp.float32), jnp.asarray(high_table, jnp.float32))


def apply_axis(signal, taps, dilation, axis_pos, direction):
    margin = 8 * dilation
    length = signal.shape[axis_pos] - 2 * margin
    result = None
    for position in range(16):
        first_cell = margin + direction * dilation * (position - 8)
        sliced = lax.slice_in_dim(signal, first_cell, first_cell + length, axis=axis_pos)
        weighted = taps[:, position][:, None, None] * sliced
        result = weighted if result is None else result + weighted
    return result


def crop(signal, amount):
    if amount == 0:
        return signal
    return signal[..., amount:-amount, amount:-amount]


def synth_level(approx, details, low_taps, high_taps, dilation):
    col_low = apply_axis(approx, low_taps, dilation, 2, -1) + apply_axis(
        details[1], high_taps, dilation, 2, -1
    )
    col_high = apply_axis(details[0], low_taps, dilation, 2, -1) + apply_axis(
        details[2], high_taps, dilation, 2, -1
    )
    return apply_axis(col_low, low_taps, dilation, 1, -1) + apply_axis(
        col_high, high_taps, dilation, 1, -1
    )


def synth_bases(bands_padded, low_taps, high_taps, start_margin):
    current = start_margin
    approx = bands_padded[:, 3 * LEVELS]
    for level_index in reversed(range(LEVELS)):
        dilation = 2**level_index
        details = [
            crop(bands_padded[:, 3 * level_index + part_index], start_margin - current)
            for part_index in range(3)
        ]
        approx = synth_level(approx, details, low_taps, high_taps, dilation)
        current = current - 8 * dilation
    return approx


def analyse(padded, low_taps, high_taps, reach):
    approx = jnp.broadcast_to(padded[None], (BASES,) + padded.shape)
    current = reach
    bands_list = []
    for level_index in range(LEVELS):
        dilation = 2**level_index
        low_rows = apply_axis(approx, low_taps, dilation, 1, 1)
        high_rows = apply_axis(approx, high_taps, dilation, 1, 1)
        current = current - 8 * dilation
        bands_list.append(crop(apply_axis(high_rows, low_taps, dilation, 2, 1), current))
        bands_list.append(crop(apply_axis(low_rows, high_taps, dilation, 2, 1), current))
        bands_list.append(crop(apply_axis(high_rows, high_taps, dilation, 2, 1), current))
        approx = apply_axis(low_rows, low_taps, dilation, 2, 1)
    bands_list.append(approx)
    return jnp.stack(bands_list, axis=1)


def on_device(iterate, gradient, dual_coeffs, weights):
    low_taps, high_taps = tap_tables()
    frame_scale = 1.0 / math.sqrt(BASES)
    reach = 8 * (2**LEVELS - 1)
    padded = with_halo(dual_coeffs, (("row", 2), ("col", 3)), reach)
    synth_total = jnp.sum(synth_bases(padded, low_taps, high_taps, reach), axis=0)
    new_image = jnp.maximum(iterate - primal_step * (gradient + frame_scale * synth_total), 0.0)
    extrapolated = 2.0 * new_image - iterate
    padded_image = with_halo(extrapolated, (("row", 0), ("col", 1)), reach)
    coeffs = frame_scale * analyse(padded_image, low_taps, high_taps, reach)
    bound_all = weights[:, :, None, None]
    return (new_image, jnp.clip(dual_coeffs + coeffs, -bound_all, bound_all))


def solution(mesh):
    return jax.shard_map(
        on_device,
        mesh=mesh,
        in_specs=(P("row", "col"), P("row", "col"), P(None, None, "row", "col"), P()),
        out_specs=(P("row", "col"), P(None, None, "row", "col")),
        check_vma=False,
    )
```

profile of v0, /device:TPU:0, one launch (start us, length us, event | category | flops | bytes accessed | tf_op | source)
XLA Modules:
  0.0 118.7 jit_solution(16544481614311725338)
XLA Ops:
  0.6 1.5 %fusion.209 = (f32[8,7,24,128]{3,2,1,0:T(8,128)S(1)}, f32[8,7,24,128]{3,2,1,0:T(8,128)S(1)}) fusion(f32[8,7,32,128]{3,2,1,0:T(8,128)} %param.8), kind=kLoop, calls=%fused_computation.456 | loop fusion | bytes 2752512 | tf_op jit(solution)/shard_map/slice | solution.py:105
  2.1 3.0 %collective-permute-start = (f32[8,7,24,128]{3,2,1,0:T(8,128)S(1)}, f32[8,7,24,128]{3,2,1,0:T(8,128)S(1)}, u32[]{:S(2)}, u32[]{:S(2)}) collective-permute-start(f32[8,7,24,128]{3,2,1,0:T(8,128)S(1)} %get-tuple-element.19), channel_id=1, source_target_pairs={{0,8},{8,16},{16,24},{24,0},{1,9},{9,17},{17,25},{25,1},{2,10},{10... | collective-permute-start | bytes 2064392 | tf_op jit(solution)/shard_map/ppermute | solution.py:104
  5.1 1.0 collective-permute-start.1
  6.1 16.2 %collective-permute-done = f32[8,7,24,128]{3,2,1,0:T(8,128)S(1)} collective-permute-done((f32[8,7,24,128]{3,2,1,0:T(8,128)S(1)}, f32[8,7,24,128]{3,2,1,0:T(8,128)S(1)}, u32[]{:S(2)}, u32[]{:S(2)}) %collective-permute-start) | collective-permute-done | bytes 688160 | tf_op jit(solution)/shard_map/ppermute | solution.py:104
  22.3 14.2 %collective-permute-done.1 = f32[8,7,24,128]{3,2,1,0:T(8,128)S(1)} collective-permute-done((f32[8,7,24,128]{3,2,1,0:T(8,128)S(1)}, f32[8,7,24,128]{3,2,1,0:T(8,128)S(1)}, u32[]{:S(2)}, u32[]{:S(2)}) %collective-permute-start.1) | collective-permute-done | bytes 688160 | tf_op jit(solution)/shard_map/ppermute | solution.py:107
  36.5 2.2 %fusion.208 = (f32[8,7,80,24]{3,2,0,1:T(8,128)}, f32[8,7,80,24]{3,2,0,1:T(8,128)S(1)}) fusion(f32[8,7,24,128]{3,2,1,0:T(8,128)S(1)} %collective-permute-done.1, f32[8,7,32,128]{3,2,1,0:T(8,128)S(1)} %copy-done, f32[8,7,24,128]{3,2,1,0:T(8,128)S(1)} %collective-permute-done), kind=kLoop, calls=%fused_computation.455 | loop fusion | flops 1146880 | bytes 3153920 | tf_op jit(solution)/shard_map/slice | solution.py:105
  38.7 3.2 %copy.69 = f32[8,7,80,24]{2,3,1,0:T(8,128)} copy(f32[8,7,80,24]{3,2,0,1:T(8,128)} %get-tuple-element.17) | data formatting | bytes 860160 | tf_op jit(solution)/shard_map/slice | solution.py:105
  41.9 1.5 %copy.70 = f32[8,7,80,24]{2,3,1,0:T(8,128)} copy(f32[8,7,80,24]{3,2,0,1:T(8,128)S(1)} %get-tuple-element.18) | data formatting | bytes 860160 | tf_op jit(solution)/shard_map/slice | solution.py:107
  43.4 3.5 %collective-permute-start.3 = (f32[8,7,80,24]{2,3,1,0:T(8,128)}, f32[8,7,80,24]{2,3,1,0:T(8,128)}, u32[]{:S(2)}, u32[]{:S(2)}) collective-permute-start(f32[8,7,80,24]{2,3,1,0:T(8,128)} %copy.70), channel_id=1, source_target_pairs={{1,0},{2,1},{3,2},{4,3},{5,4},{6,5},{7,6},{0,7},{9,8},{10,9},{11,1... | collective-permute-start | bytes 1290248 | tf_op jit(solution)/shard_map/ppermute | solution.py:107
  47.2 11.0 %collective-permute-done.2 = f32[8,7,80,24]{2,3,1,0:T(8,128)} collective-permute-done((f32[8,7,80,24]{2,3,1,0:T(8,128)}, f32[8,7,80,24]{2,3,1,0:T(8,128)}, u32[]{:S(2)}, u32[]{:S(2)}) %collective-permute-start.2) | collective-permute-done | bytes 430112 | tf_op jit(solution)/shard_map/ppermute | solution.py:104
  58.1 1.8 %copy.71 = f32[8,7,80,24]{3,2,0,1:T(8,128)S(1)} copy(f32[8,7,80,24]{2,3,1,0:T(8,128)} %collective-permute-done.2) | data formatting | bytes 860160 | tf_op jit(solution)/shard_map/ppermute | solution.py:104
  59.9 3.2 %copy.72 = f32[8,7,80,24]{3,2,0,1:T(8,128)} copy(f32[8,7,80,24]{2,3,1,0:T(8,128)} %collective-permute-done.3) | data formatting | bytes 860160 | tf_op jit(solution)/shard_map/ppermute | solution.py:107
  63.1 3.8 %pad_maximum_fusion = f32[8,7,80,176]{3,2,0,1:T(8,128)S(1)} fusion(f32[8,7,80,24]{3,2,0,1:T(8,128)} %copy.72, f32[8,7,80,24]{3,2,0,1:T(8,128)S(1)} %copy.71, f32[8,7,24,128]{3,2,1,0:T(8,128)} %copy-done.2, f32[8,7,32,128]{3,2,1,0:T(8,128)S(1)} %copy-done, f32[8,7,24,128]{3,2,1,0:T(8,128)} %copy-done.1), kind=kLoop, calls=%fused_computation | loop fusion | flops 2723840 | bytes 6307840 | tf_op jit(solution)/shard_map/concatenate | solution.py:108
  68.1 7.2 %fusion.32 = f32[8,80,144]{2,1,0:T(8,128)S(1)} fusion(f32[8,80,176]{2,1,0:T(8,128)S(1)} %get-tuple-element.16, f32[8,80,176]{2,1,0:T(8,128)S(1)} %get-tuple-element.10, f32[8]{0:T(128)S(1)} %copy-done.31, f32[8]{0:T(128)S(1)} %copy-done.30, f32[8]{0:T(128)S(1)} %copy-done.29, f32[8]{0:T(128)S(1)} %copy-done.28, f32[8]{0:T(128)S(1)} %copy-done.27, ...), kind=kLoop, calls=%fused_computation.73 | loop fusion | flops 5806080 | bytes 12166112 | tf_op jit(solution)/shard_map/add | solution.py:147
  75.2 7.0 %fusion.1 = f32[8,80,144]{2,1,0:T(8,128)S(1)} fusion(f32[8,80,176]{2,1,0:T(8,128)S(1)} %get-tuple-element.14, f32[8,80,176]{2,1,0:T(8,128)S(1)} %get-tuple-element.15, f32[8]{0:T(128)S(1)} %copy-done.31, f32[8]{0:T(128)S(1)} %copy-done.30, f32[8]{0:T(128)S(1)} %copy-done.29, f32[8]{0:T(128)S(1)} %copy-done.28, f32[8]{0:T(128)S(1)} %copy-done.27, ...), kind=kLoop, calls=%fused_computation.8 | loop fusion | flops 5806080 | bytes 12166112 | tf_op jit(solution)/shard_map/add | solution.py:150
  82.3 1.7 %fusion.63 = f32[8,48,144]{2,1,0:T(8,128)S(1)} fusion(f32[8,80,144]{2,1,0:T(8,128)S(1)} %fusion.1, f32[8,80,144]{2,1,0:T(8,128)S(1)} %fusion.32, f32[8]{0:T(128)S(1)} %copy-done.31, f32[8]{0:T(128)S(1)} %copy-done.30, f32[8]{0:T(128)S(1)} %copy-done.29, f32[8]{0:T(128)S(1)} %copy-done.28, f32[8]{0:T(128)S(1)} %copy-done.27, f32[8]{0:T(128)S(1)} %copy-done.33, ...), kind=kLoop, calls=%fused_computation.147 | loop fusion | flops 3483648 | bytes 7300064 | tf_op jit(solution)/shard_map/add | solution.py:153
  84.0 2.3 %fusion.125 = f32[8,48,128]{2,1,0:T(8,128)S(1)} fusion(f32[8,80,176]{2,1,0:T(8,128)S(1)} %get-tuple-element.13, f32[8,48,144]{2,1,0:T(8,128)S(1)} %fusion.63, f32[8]{0:T(128)S(1)} %copy-done.31, f32[8]{0:T(128)S(1)} %copy-done.30, f32[8]{0:T(128)S(1)} %copy-done.29, f32[8]{0:T(128)S(1)} %copy-done.28, f32[8]{0:T(128)S(1)} %copy-done.27, ...), kind=kLoop, calls=%fused_computation.275 | loop fusion | flops 3096576 | bytes 6489056 | tf_op jit(solution)/shard_map/add | solution.py:147
  86.3 2.3 %fusion.94 = f32[8,48,128]{2,1,0:T(8,128)S(1)} fusion(f32[8,80,176]{2,1,0:T(8,128)S(1)} %get-tuple-element.11, f32[8,80,176]{2,1,0:T(8,128)S(1)} %get-tuple-element.12, f32[8]{0:T(128)S(1)} %copy-done.31, f32[8]{0:T(128)S(1)} %copy-done.30, f32[8]{0:T(128)S(1)} %copy-done.29, f32[8]{0:T(128)S(1)} %copy-done.28, f32[8]{0:T(128)S(1)} %copy-done.27, ...), kind=kLoop, calls=%fused_computation.212 | loop fusion | flops 3096576 | bytes 6489056 | tf_op jit(solution)/shard_map/add | solution.py:150
  89.3 1.5 %collective-permute-start.4 = (f32[24,128]{0,1:T(8,128)S(1)}, f32[24,128]{0,1:T(8,128)S(1)}, u32[]{:S(2)}, u32[]{:S(2)}) collective-permute-start(f32[24,128]{0,1:T(8,128)S(1)} %get-tuple-element.52), channel_id=1, source_target_pairs={{0,8},{8,16},{16,24},{24,0},{1,9},{9,17},{17,25},{25,1},{2,10},{10... | collective-permute-start | bytes 36872 | tf_op jit(solution)/shard_map/ppermute | solution.py:104
  90.9 1.4 %collective-permute-start.5 = (f32[24,128]{0,1:T(8,128)S(1)}, f32[24,128]{0,1:T(8,128)S(1)}, u32[]{:S(2)}, u32[]{:S(2)}) collective-permute-start(f32[24,128]{0,1:T(8,128)S(1)} %get-tuple-element.53), channel_id=1, source_target_pairs={{8,0},{16,8},{24,16},{0,24},{9,1},{17,9},{25,17},{1,25},{10,2},{18... | collective-permute-start | bytes 36872 | tf_op jit(solution)/shard_map/ppermute | solution.py:107
  92.3 2.2 %collective-permute-done.4 = f32[24,128]{0,1:T(8,128)S(1)} collective-permute-done((f32[24,128]{0,1:T(8,128)S(1)}, f32[24,128]{0,1:T(8,128)S(1)}, u32[]{:S(2)}, u32[]{:S(2)}) %collective-permute-start.4) | collective-permute-done | bytes 12320 | tf_op jit(solution)/shard_map/ppermute | solution.py:104
  94.5 0.9 collective-permute-done.5
  95.8 3.2 %collective-permute-start.7 = (f32[80,24]{0,1:T(8,128)S(1)}, f32[80,24]{0,1:T(8,128)S(1)}, u32[]{:S(2)}, u32[]{:S(2)}) collective-permute-start(f32[80,24]{0,1:T(8,128)S(1)} %get-tuple-element.35), channel_id=1, source_target_pairs={{1,0},{2,1},{3,2},{4,3},{5,4},{6,5},{7,6},{0,7},{9,8},{10,9},{11,1... | collective-permute-start | bytes 23048 | tf_op jit(solution)/shard_map/ppermute | solution.py:107
  103.7 1.4 %multiply_add_fusion.4 = f32[8,64,160]{2,1,0:T(8,128)S(1)} fusion(f32[8,64,176]{2,1,0:T(8,128)S(1)} %multiply_add_fusion.5, f32[8]{0:T(128)S(1)} %copy-done.13, f32[8]{0:T(128)S(1)} %copy-done.12, f32[8]{0:T(128)S(1)} %copy-done.11, f32[8]{0:T(128)S(1)} %copy-done.10, f32[8]{0:T(128)S(1)} %copy-done.9, f32[8]{0:T(128)S(1)} %copy-done.8, f32[8]{0:T(128)S(1)} %copy-done.7, ...), kind=kLoop, calls=%fused_computation.140 | loop fusion | flops 1556480 | bytes 3604800 | tf_op jit(solution)/shard_map/add | solution.py:136
  105.2 1.7 %slice_multiply_fusion.65 = (f32[8,64,160]{2,1,0:T(8,128)S(1)}, f32[8,64,160]{2,1,0:T(8,128)S(1)}, f32[8,64,160]{2,1,0:T(8,128)S(1)}, f32[8,64,160]{2,1,0:T(8,12...) fusion(f32[8,64,176]{2,1,0:T(8,128)S(1)} %multiply_add_fusion.5, ...), kind=kLoop, calls=%fused_computation.143 | loop fusion | flops 245760 | bytes 8192064 | tf_op jit(solution)/shard_map/mul | solution.py:135
  106.9 1.4 %multiply_add_fusion.2 = f32[8,64,160]{2,1,0:T(8,128)S(1)} fusion(f32[8,64,176]{2,1,0:T(8,128)S(1)} %multiply_add_fusion.3, f32[8]{0:T(128)S(1)} %copy-done.26, f32[8]{0:T(128)S(1)} %copy-done.25, f32[8]{0:T(128)S(1)} %copy-done.24, f32[8]{0:T(128)S(1)} %copy-done.23, f32[8]{0:T(128)S(1)} %copy-done.22, f32[8]{0:T(128)S(1)} %copy-done.21, ...), kind=kLoop, calls=%fused_computation.138 | loop fusion | flops 1556480 | bytes 3604800 | tf_op jit(solution)/shard_map/add | solution.py:136
  108.3 1.4 %multiply_add_fusion.1 = f32[8,64,160]{2,1,0:T(8,128)S(1)} fusion(f32[8,64,176]{2,1,0:T(8,128)S(1)} %multiply_add_fusion.5, f32[8]{0:T(128)S(1)} %copy-done.26, f32[8]{0:T(128)S(1)} %copy-done.25, f32[8]{0:T(128)S(1)} %copy-done.24, f32[8]{0:T(128)S(1)} %copy-done.23, f32[8]{0:T(128)S(1)} %copy-done.22, f32[8]{0:T(128)S(1)} %copy-done.21, ...), kind=kLoop, calls=%fused_computation.137 | loop fusion | flops 1556480 | bytes 3604800 | tf_op jit(solution)/shard_map/add | solution.py:136
  109.7 2.5 %multiply_add_fusion = f32[8,64,160]{2,1,0:T(8,128)S(1)} fusion(f32[8,64,176]{2,1,0:T(8,128)S(1)} %multiply_add_fusion.3, f32[8]{0:T(128)S(1)} %copy-done.3, f32[8]{0:T(128)S(1)} %copy-done.17, f32[8]{0:T(128)S(1)} %copy-done.16, f32[8]{0:T(128)S(1)} %copy-done.15, f32[8]{0:T(128)S(1)} %copy-done.14, f32[8]{0:T(128)S(1)} %copy-done.32, f32[8]{0:T(128)S(1)} %copy-done.13, ...), kind=kLoop, calls=%fused_computation.136 | loop fusion | flops 2539520 | bytes 5571072 | tf_op jit(solution)/shard_map/add | solution.py:136
  114.2 1.0 bitcast_dynamic-update-slice_fusion.3
  115.2 0.8 bitcast_dynamic-update-slice_fusion.2
  116.8 0.8 bitcast_dynamic-update-slice_fusion
  117.5 1.2 maximum_minimum_fusion
  (115 shorter events, 9.3 us)
Async XLA Ops:
  0.6 35.9 %copy-start = (f32[8,7,32,128]{3,2,1,0:T(8,128)S(1)}, f32[8,7,32,128]{3,2,1,0:T(8,128)}, u32[]{:S(2)}) copy-start(f32[8,7,32,128]{3,2,1,0:T(8,128)} %param.8) | copy-start | bytes 2752516
  2.1 20.2 %collective-permute-start = (f32[8,7,24,128]{3,2,1,0:T(8,128)S(1)}, f32[8,7,24,128]{3,2,1,0:T(8,128)S(1)}, u32[]{:S(2)}, u32[]{:S(2)}) collective-permute-start(f32[8,7,24,128]{3,2,1,0:T(8,128)S(1)} %get-tuple-element.19), channel_id=1, source_target_pairs={{0,8},{8,16},{16,24},{24,0},{1,9},{9,17},{17,25},{25,1},{2,10},{10... | collective-permute-start | bytes 2064392 | tf_op jit(solution)/shard_map/ppermute | solution.py:104
  5.1 31.4 %collective-permute-start.1 = (f32[8,7,24,128]{3,2,1,0:T(8,128)S(1)}, f32[8,7,24,128]{3,2,1,0:T(8,128)S(1)}, u32[]{:S(2)}, u32[]{:S(2)}) collective-permute-start(f32[8,7,24,128]{3,2,1,0:T(8,128)S(1)} %get-tuple-element.20), channel_id=1, source_target_pairs={{8,0},{16,8},{24,16},{0,24},{9,1},{17,9},{25,17},{1,25},{10,2},{18... | collective-permute-start | bytes 2064392 | tf_op jit(solution)/shard_map/ppermute | solution.py:107
  22.3 16.4 %copy-start.1 = (f32[8,7,24,128]{3,2,1,0:T(8,128)}, f32[8,7,24,128]{3,2,1,0:T(8,128)S(1)}, u32[]{:S(2)}) copy-start(f32[8,7,24,128]{3,2,1,0:T(8,128)S(1)} %collective-permute-done) | copy-start | bytes 2064388
  36.5 2.2 %copy-start.2 = (f32[8,7,24,128]{3,2,1,0:T(8,128)}, f32[8,7,24,128]{3,2,1,0:T(8,128)S(1)}, u32[]{:S(2)}) copy-start(f32[8,7,24,128]{3,2,1,0:T(8,128)S(1)} %collective-permute-done.1) | copy-start | bytes 2064388
  38.7 8.2 %copy-start.35 = (f32[32,128]{1,0:T(8,128)S(1)}, f32[32,128]{1,0:T(8,128)}, u32[]{:S(2)}) copy-start(f32[32,128]{1,0:T(8,128)} %param.7) | copy-start | bytes 49156
  38.7 8.3 %copy-start.36 = (f32[32,128]{1,0:T(8,128)S(1)}, f32[32,128]{1,0:T(8,128)}, u32[]{:S(2)}) copy-start(f32[32,128]{1,0:T(8,128)} %param.6) | copy-start | bytes 49156
  41.9 16.2 %collective-permute-start.2 = (f32[8,7,80,24]{2,3,1,0:T(8,128)}, f32[8,7,80,24]{2,3,1,0:T(8,128)}, u32[]{:S(2)}, u32[]{:S(2)}) collective-permute-start(f32[8,7,80,24]{2,3,1,0:T(8,128)} %copy.69), channel_id=1, source_target_pairs={{0,1},{1,2},{2,3},{3,4},{4,5},{5,6},{6,7},{7,0},{8,9},{9,10},{10,1... | collective-permute-start | bytes 1290248 | tf_op jit(solution)/shard_map/ppermute | solution.py:104
  43.4 16.5 %collective-permute-start.3 = (f32[8,7,80,24]{2,3,1,0:T(8,128)}, f32[8,7,80,24]{2,3,1,0:T(8,128)}, u32[]{:S(2)}, u32[]{:S(2)}) collective-permute-start(f32[8,7,80,24]{2,3,1,0:T(8,128)} %copy.70), channel_id=1, source_target_pairs={{1,0},{2,1},{3,2},{4,3},{5,4},{6,5},{7,6},{0,7},{9,8},{10,9},{11,1... | collective-permute-start | bytes 1290248 | tf_op jit(solution)/shard_map/ppermute | solution.py:107
  66.9 0.9 copy-start.3
  66.9 0.9 copy-start.4
  66.9 0.9 copy-start.5
  66.9 0.9 copy-start.6
  66.9 0.9 copy-start.7
  67.0 0.9 copy-start.8
  67.0 0.8 copy-start.9
  67.0 0.8 copy-start.10
  67.0 0.8 copy-start.11
  67.0 0.8 copy-start.12
  67.0 0.8 copy-start.13
  67.0 0.8 copy-start.14
  67.0 0.8 copy-start.15
  67.1 0.8 copy-start.16
  67.1 0.8 copy-start.17
  67.1 0.8 copy-start.18
  67.1 0.8 copy-start.19
  67.1 0.8 copy-start.20
  88.6 10.5 %copy-start.34 = (f32[8,7]{1,0:T(8,128)S(1)}, f32[8,7]{1,0:T(8,128)}, u32[]{:S(2)}) copy-start(f32[8,7]{1,0:T(8,128)} %param.9) | copy-start | bytes 676
  89.3 5.2 %collective-permute-start.4 = (f32[24,128]{0,1:T(8,128)S(1)}, f32[24,128]{0,1:T(8,128)S(1)}, u32[]{:S(2)}, u32[]{:S(2)}) collective-permute-start(f32[24,128]{0,1:T(8,128)S(1)} %get-tuple-element.52), channel_id=1, source_target_pairs={{0,8},{8,16},{16,24},{24,0},{1,9},{9,17},{17,25},{25,1},{2,10},{10... | collective-permute-start | bytes 36872 | tf_op jit(solution)/shard_map/ppermute | solution.py:104
  90.9 4.6 %collective-permute-start.5 = (f32[24,128]{0,1:T(8,128)S(1)}, f32[24,128]{0,1:T(8,128)S(1)}, u32[]{:S(2)}, u32[]{:S(2)}) collective-permute-start(f32[24,128]{0,1:T(8,128)S(1)} %get-tuple-element.53), channel_id=1, source_target_pairs={{8,0},{16,8},{24,16},{0,24},{9,1},{17,9},{25,17},{1,25},{10,2},{18... | collective-permute-start | bytes 36872 | tf_op jit(solution)/shard_map/ppermute | solution.py:107
  95.5 5.0 %collective-permute-start.6 = (f32[80,24]{0,1:T(8,128)S(1)}, f32[80,24]{0,1:T(8,128)S(1)}, u32[]{:S(2)}, u32[]{:S(2)}) collective-permute-start(f32[80,24]{0,1:T(8,128)S(1)} %get-tuple-element.34), channel_id=1, source_target_pairs={{0,1},{1,2},{2,3},{3,4},{4,5},{5,6},{6,7},{7,0},{8,9},{9,10},{10,1... | collective-permute-start | bytes 23048 | tf_op jit(solution)/shard_map/ppermute | solution.py:104
  95.8 4.6 %collective-permute-start.7 = (f32[80,24]{0,1:T(8,128)S(1)}, f32[80,24]{0,1:T(8,128)S(1)}, u32[]{:S(2)}, u32[]{:S(2)}) collective-permute-start(f32[80,24]{0,1:T(8,128)S(1)} %get-tuple-element.35), channel_id=1, source_target_pairs={{1,0},{2,1},{3,2},{4,3},{5,4},{6,5},{7,6},{0,7},{9,8},{10,9},{11,1... | collective-permute-start | bytes 23048 | tf_op jit(solution)/shard_map/ppermute | solution.py:107
  (13 other events, 10.4 us)
where the time goes:
time: 119 us
  waiting for transfers between devices  45.2 us (38%)
  other arithmetic  43.4 us (36%)
  local copies, waits for them, and re-layouts  14.5 us (12%)
  starting transfers between devices  14.1 us (12%)
  between operations  1.47 us (1%)
    ppermute x4, waiting for transfers between devices, with_halo(): lax.ppermute(lax.slice_in_dim(block, block.shape[dim] - width, None, axis...  30.1 us
    ppermute x4, waiting for transfers between devices, with_halo(): lax.ppermute(lax.slice_in_dim(block, 0, width, axis=dim), axis, backward)  15.1 us
    add x2, other arithmetic, synth_level(): apply_axis(approx, low_taps, dilation, 2, -1)  9.48 us
    add x2, other arithmetic, synth_level(): apply_axis(details[0], low_taps, dilation, 2, -1)  9.29 us
    ppermute x4, starting transfers between devices, with_halo(): lax.ppermute(lax.slice_in_dim(block, 0, width, axis=dim), axis, backward)  9.24 us
    add x8, other arithmetic, apply_axis(): result = weighted if result is None else result + weighted  9 us
    ppermute x4, starting transfers between devices, with_halo(): lax.ppermute(lax.slice_in_dim(block, block.shape[dim] - width, None, axis...  4.82 us
    slice x3, local copies, waits for them, and re-layouts, with_halo(): lax.slice_in_dim(block, block.shape[dim] - width, None, axis=dim)  4.77 us
  transfers between devices with their start and end apart: 8, of which 6 were waited for; matrix products, arithmetic and copies ran while one was open for 3% of the time, Pallas kernels for 0%

commit v1 on v0

v1 whole, which is shorter than its diff:
```python
import functools
import math

import jax
import jax.numpy as jnp
import ml_dtypes
import numpy as np
from jax import lax
from jax.experimental import pallas as pl
from jax.experimental.pallas import tpu as pltpu
from jax.sharding import PartitionSpec as P

BASES = 8
BANDS = 7
REACH = 24
MESH = pl.DeviceIdType.MESH

primal_step = 0.5

daubechies_table = [
    [0.7071067811865476, 0.7071067811865476],
    [0.48296291314469025, 0.836516303737469, 0.22414386804185735, -0.12940952255092145],
    [
        0.3326705529509569,
        0.8068915093133388,
        0.4598775021193313,
        -0.13501102001039084,
        -0.08544127388224149,
        0.035226291882100656,
    ],
    [
        0.23037781330885523,
        0.7148465705525415,
        0.6308807679295904,
        -0.02798376941698385,
        -0.18703481171888114,
        0.030841381835986965,
        0.032883011666982945,
        -0.010597401784997278,
    ],
    [
        0.160102397974125,
        0.6038292697974729,
        0.7243085284385744,
        0.13842814590110342,
        -0.24229488706619015,
        -0.03224486958502952,
        0.07757149384006515,
        -0.006241490213011705,
        -0.012580751999015526,
        0.003335725285001549,
    ],
    [
        0.11154074335008017,
        0.4946238903983854,
        0.7511339080215775,
        0.3152503517092432,
        -0.22626469396516913,
        -0.12976686756709563,
        0.09750160558707936,
        0.02752286553001629,
        -0.031582039318031156,
        0.0005538422009938016,
        0.004777257511010651,
        -0.00107730108499558,
    ],
    [
        0.07785205408506236,
        0.39653931948230575,
        0.7291320908465551,
        0.4697822874053586,
        -0.14390600392910627,
        -0.22403618499416572,
        0.07130921926705004,
        0.0806126091510659,
        -0.03802993693503463,
        -0.01657454163101562,
        0.012550998556013784,
        0.00042957797300470274,
        -0.0018016407039998328,
        0.0003537138000010399,
    ],
    [
        0.05441584224308161,
        0.3128715909144659,
        0.6756307362980128,
        0.5853546836548691,
        -0.015829105256023893,
        -0.2840155429624281,
        0.00047248457399797254,
        0.128747426620186,
        -0.01736930100202211,
        -0.04408825393106472,
        0.013981027917015516,
        0.008746094047015655,
        -0.00487035299301066,
        -0.0003917403729959771,
        0.0006754494059985568,
        -0.00011747678400228192,
    ],
]


def tap_pairs(basis):
    taps = np.array(daubechies_table[basis])
    low = taps / np.sum(taps)
    high = np.array([(-1.0) ** t * low[len(low) - 1 - t] for t in range(len(low))])
    return low, high


def composite(basis):
    low, high = tap_pairs(basis)
    n = len(low) // 2
    fine = [{t - n: f[t] for t in range(2 * n)} for f in (low, high)]
    both = []
    for f in (low, high):
        out = {}
        for s in range(2 * n):
            for t in range(2 * n):
                off = (s - n) + 2 * (t - n)
                out[off] = out.get(off, 0.0) + low[s] * f[t]
        both.append(out)
    return fine + both


def halves(matrix):
    high = matrix.astype(np.float32).astype(ml_dtypes.bfloat16)
    low = (matrix - high.astype(np.float64)).astype(np.float32).astype(ml_dtypes.bfloat16)
    return np.stack([high, low])


@functools.lru_cache(maxsize=None)
def matrices(h, w):
    span = h + 2 * REACH
    scale = 1.0 / math.sqrt(BASES)
    a = np.zeros((BASES, 4 * span, BANDS * h))
    b = np.zeros((BASES, BANDS * h, 2 * span))
    c = np.zeros((BASES, 4 * w, 2 * w))
    kinds = [(1, 0), (0, 1), (1, 1), (3, 2), (2, 3), (3, 3), (2, 2)]
    for basis in range(BASES):
        filters = composite(basis)
        rows = np.zeros((4, h, span))
        for kind in range(4):
            for off, tap in filters[kind].items():
                for j in range(h):
                    rows[kind, j, j + REACH + off] += scale * tap
                for j in range(w):
                    c[basis, kind * w + j, (j + off) % (2 * w)] += tap
        for band, (row_kind, col_kind) in enumerate(kinds):
            mat = rows[row_kind]
            a[basis, col_kind * span : (col_kind + 1) * span, band * h : (band + 1) * h] = mat.T
            at = col_kind % 2
            b[basis, band * h : (band + 1) * h, at * span : (at + 1) * span] = mat
    return halves(a), halves(b), halves(c)


def split(x):
    high = x.astype(jnp.bfloat16)
    low = (x - high.astype(jnp.float32)).astype(jnp.bfloat16)
    return high, low


def left_dot(m_high, m_low, x):
    width = x.shape[1]
    high, low = split(x)
    pair = jnp.dot(
        m_high, jnp.concatenate([high, low], axis=1), preferred_element_type=jnp.float32
    )
    rest = jnp.dot(m_low, high, preferred_element_type=jnp.float32)
    return pair[:, :width] + (pair[:, width:] + rest)


def synth_one(x, a_ref, c_ref, h, w):
    span = h + 2 * REACH
    z = left_dot(a_ref[0, 0], a_ref[1, 0], x)
    z = jnp.concatenate([z[k * span : (k + 1) * span] for k in range(4)], axis=1)
    high, low = split(z)
    pair = jnp.dot(
        jnp.concatenate([high, low], axis=0), c_ref[0, 0], preferred_element_type=jnp.float32
    )
    rest = jnp.dot(high, c_ref[1, 0], preferred_element_type=jnp.float32)
    return pair[:span] + (pair[span:] + rest)


def partners():
    return [(dr, dc) for dr in (-2, -1, 0, 1, 2) for dc in (-1, 0, 1) if (dr, dc) != (0, 0)]


def near():
    return [(dr, dc) for dr in (-1, 0, 1) for dc in (-1, 0, 1) if (dr, dc) != (0, 0)]


def overlap(dr, h):
    span = h + 2 * REACH
    shift = h * abs(dr)
    return (shift, 0, span - shift) if dr > 0 else (0, shift, span - shift)


def border(dr, h):
    if dr == 0:
        return (REACH, REACH, h)
    return (h, 0, REACH) if dr > 0 else (REACH, h + REACH, REACH)


def primal_kernel(
    it_ref, gr_ref, x_ref, a_ref, c_ref, e_ref, img_ref,
    acc, held, slots, side, sides_in, bar_sent, bar_recv, send, recv,
):
    h, w = it_ref.shape
    span = h + 2 * REACH
    step = pl.program_id(0)
    nrow, ncol = lax.axis_size("row"), lax.axis_size("col")
    row, col = lax.axis_index("row"), lax.axis_index("col")

    def device(dr, dc):
        return (lax.rem(row + dr + 2 * nrow, nrow), lax.rem(col + dc + ncol, ncol))

    def held_copy(i, dr, dc):
        here, there, rows = border(dr, h)
        return pltpu.make_async_remote_copy(
            src_ref=held.at[1, pl.ds(here, rows)],
            dst_ref=held.at[1 + dc if dc else 3, pl.ds(there, rows)],
            send_sem=bar_sent.at[i], recv_sem=bar_recv.at[i],
            device_id=device(dr, dc), device_id_type=MESH,
        )

    def sum_copy(i, dr, dc):
        here, there, rows = overlap(dr, h)
        slot = dr + 2
        if dc == 0:
            src = acc.at[pl.ds(here, rows)]
            dst = slots.at[slot, pl.ds(there, rows)]
        else:
            src = side.at[(dc + 1) // 2, pl.ds(here, rows)]
            dst = sides_in.at[(dc + 1) // 2, slot, pl.ds(there, rows)]
        return pltpu.make_async_remote_copy(
            src_ref=src, dst_ref=dst, send_sem=send.at[i], recv_sem=recv.at[i],
            device_id=device(dr, dc), device_id_type=MESH,
        )

    @pl.when(step == 0)
    def _():
        barrier = pltpu.get_barrier_semaphore()
        for dr, dc in partners():
            pl.semaphore_signal(barrier, inc=1, device_id=device(dr, dc), device_id_type=MESH)
        held[1, REACH : REACH + h] = it_ref[...]
        acc[...] = jnp.zeros_like(acc)
        acc[REACH : REACH + h, :w] = it_ref[...] - primal_step * gr_ref[...]
        pl.semaphore_wait(barrier, len(partners()))
        for i, (dr, dc) in enumerate(near()):
            held_copy(i, dr, dc).start()

    acc[...] += -primal_step * synth_one(x_ref[0], a_ref, c_ref, h, w)

    @pl.when(step == BASES - 1)
    def _():
        left = lax.broadcasted_iota(jnp.int32, (span, w), 1) < w // 2
        mine, over = acc[:, :w], acc[:, w:]
        side[0] = jnp.where(left, mine, over)
        side[1] = jnp.where(left, over, mine)
        for i, (dr, dc) in enumerate(partners()):
            sum_copy(i, dr, dc).start()
        for i, (dr, dc) in enumerate(near()):
            held_copy(i, dr, dc).wait()
        for i, (dr, dc) in enumerate(partners()):
            sum_copy(i, dr, dc).wait()

        def gather(read, start):
            total = start
            for dr in (-2, -1, 0, 1, 2):
                if dr == 0 and start is not None:
                    continue
                _, there, rows = overlap(dr, h)
                part = read(dr + 2, there, rows)
                sizes = (there, span - there - rows)
                above, below = [jnp.zeros((n, part.shape[1]), jnp.float32) for n in sizes]
                blocks = [above] * (there > 0) + [part] + [below] * (sizes[1] > 0)
                part = jnp.concatenate(blocks, axis=0) if len(blocks) > 1 else part
                total = part if total is None else total + part
            return total

        mid = gather(lambda s, t, n: slots[s, t : t + n], acc[...])
        from_right = gather(lambda s, t, n: sides_in[0, s, t : t + n], None)
        from_left = gather(lambda s, t, n: sides_in[1, s, t : t + n], None)
        inner = mid[:, :w] + jnp.where(left, from_left, from_right)
        outer = mid[:, w:] + jnp.where(left, from_right, from_left)
        inner = jnp.maximum(inner, 0.0)
        outer = jnp.maximum(outer, 0.0)
        img_ref[...] = inner[REACH : REACH + h]
        it_inner = jnp.concatenate(
            [held[3, :REACH], held[1, REACH : REACH + h], held[3, REACH + h :]], axis=0
        )
        it_outer = jnp.where(left, held[0], held[2])
        ext = jnp.concatenate([2.0 * inner - it_inner, 2.0 * outer - it_outer], axis=1)
        high, low = split(ext)
        e_ref[:span] = high
        e_ref[span:] = low


def dual_kernel(wt_ref, e_ref, img_ref, x_ref, b_ref, c_ref, img_out, x_out):
    h, w = img_ref.shape
    span = h + 2 * REACH
    step = pl.program_id(0)

    @pl.when(step == 0)
    def _():
        img_out[...] = img_ref[...]

    across = (((1,), (1,)), ((), ()))
    pair = lax.dot_general(e_ref[...], c_ref[0, 0], across, preferred_element_type=jnp.float32)
    rest = lax.dot_general(
        e_ref[:span], c_ref[1, 0], across, preferred_element_type=jnp.float32
    )
    z = pair[:span] + (pair[span:] + rest)
    for first, last, at in ((0, 3, 0), (3, 7, 2)):
        data = jnp.concatenate(
            [z[:, at * w : (at + 1) * w], z[:, (at + 1) * w : (at + 2) * w]], axis=0
        )
        rows = slice(first * h, last * h)
        coeffs = left_dot(b_ref[0, 0, rows], b_ref[1, 0, rows], data)
        for band in range(first, last):
            bound = wt_ref[step, band]
            value = x_ref[0, band * h : (band + 1) * h]
            value = value + coeffs[(band - first) * h : (band - first + 1) * h]
            x_out[0, band * h : (band + 1) * h] = jnp.clip(value, -bound, bound)


def on_device(iterate, gradient, dual_coeffs, weights):
    h, w = iterate.shape
    span = h + 2 * REACH
    a, b, c = [jnp.asarray(m) for m in matrices(h, w)]
    duals = dual_coeffs.reshape(BASES, BANDS * h, w)
    whole = pl.BlockSpec((h, w), lambda i: (0, 0))
    per_basis = pl.BlockSpec((1, BANDS * h, w), lambda i: (i, 0, 0))
    halved = lambda m: pl.BlockSpec((2, 1) + m.shape[2:], lambda i: (0, i, 0, 0))
    ext, image = pl.pallas_call(
        primal_kernel,
        grid=(BASES,),
        out_shape=(
            jax.ShapeDtypeStruct((2 * span, 2 * w), jnp.bfloat16),
            jax.ShapeDtypeStruct((h, w), jnp.float32),
        ),
        in_specs=[whole, whole, per_basis, halved(a), halved(c)],
        out_specs=(pl.BlockSpec((2 * span, 2 * w), lambda i: (0, 0)), whole),
        scratch_shapes=[
            pltpu.VMEM((span, 2 * w), jnp.float32),
            pltpu.VMEM((4, span, w), jnp.float32),
            pltpu.VMEM((5, span, 2 * w), jnp.float32),
            pltpu.VMEM((2, span, w), jnp.float32),
            pltpu.VMEM((2, 5, span, w), jnp.float32),
            pltpu.SemaphoreType.DMA((8,)),
            pltpu.SemaphoreType.DMA((8,)),
            pltpu.SemaphoreType.DMA((14,)),
            pltpu.SemaphoreType.DMA((14,)),
        ],
        compiler_params=pltpu.CompilerParams(
            collective_id=0, has_side_effects=True, vmem_limit_bytes=24 * 2**20
        ),
    )(iterate, gradient, duals, a, c)
    new_image, new_duals = pl.pallas_call(
        dual_kernel,
        grid=(BASES,),
        out_shape=(
            jax.ShapeDtypeStruct((h, w), jnp.float32),
            jax.ShapeDtypeStruct(duals.shape, jnp.float32),
        ),
        in_specs=[
            pl.BlockSpec(memory_space=pltpu.SMEM),
            pl.BlockSpec((2 * span, 2 * w), lambda i: (0, 0)),
            whole,
            per_basis,
            halved(b),
            halved(c),
        ],
        out_specs=(whole, per_basis),
        compiler_params=pltpu.CompilerParams(vmem_limit_bytes=24 * 2**20),
    )(weights, ext, image, duals, b, c)
    return new_image, new_duals.reshape(dual_coeffs.shape)


def solution(mesh):
    return jax.shard_map(
        on_device,
        mesh=mesh,
        in_specs=(P("row", "col"), P("row", "col"), P(None, None, "row", "col"), P()),
        out_specs=(P("row", "col"), P(None, None, "row", "col")),
        check_vma=False,
    )
```

time: 119 us -> 29.5 us (0.25)
  waiting for transfers between devices: 45.2 us -> 0 us
  other arithmetic: 43.4 us -> 0 us
  Pallas kernels: 0 us -> 21.9 us
  starting transfers between devices: 14.1 us -> 0 us
  local copies, waits for them, and re-layouts: 14.5 us -> 6.55 us
    ppermute x8 -> x0, waiting for transfers between devices: 45.2 us -> none  [the longest x4 30.1 us: with_halo(): lax.ppermute(lax.slice_in_dim(block, block.shape[dim] - width, None, axis...]
    add x13 -> x0, other arithmetic: 29.5 us -> none  [the longest x2 9.48 us: synth_level(): apply_axis(approx, low_taps, dilation, 2, -1)]
    pallas_call x0 -> x2, Pallas kernels: none -> 21.9 us  [the longest x1 15.9 us: on_device(): pl.pallas_call(primal_kernel, grid=(BASES,), out_shape=(jax.ShapeDtypeStr...]
    ppermute x8 -> x0, starting transfers between devices: 14.1 us -> none  [the longest x4 9.24 us: with_halo(): lax.ppermute(lax.slice_in_dim(block, 0, width, axis=dim), axis, backward)]
    slice x21 -> x0, local copies, waits for them, and re-layouts: 7.92 us -> none  [the longest x3 4.77 us: with_halo(): lax.slice_in_dim(block, block.shape[dim] - width, None, axis=dim)]
    unnamed x78 -> x16, local copies, waits for them, and re-layouts: 1.21 us -> 6.55 us
    ppermute x2 -> x0, local copies, waits for them, and re-layouts: 4.92 us -> none  [the longest x1 3.16 us: with_halo(): lax.ppermute(lax.slice_in_dim(block, 0, width, axis=dim), axis, backward)]
    concatenate x1 -> x0, other arithmetic: 3.83 us -> none  [with_halo(): block = jnp.concatenate([low, block, high], axis=dim)]
  transfers between devices with their start and end apart: 8 -> 0, of which waited for: 6 -> 0; matrix products, arithmetic and copies ran while one was open for 3% -> 0% of each run, Pallas kernels for 0% -> 0%
where the time goes in v1:
time: 29.5 us; the launch traced here: 29.1 us
  Pallas kernels  21.9 us (74%)
  local copies, waits for them, and re-layouts  6.55 us (22%)
  between operations  0.68 us (2%)
    pallas_call x1, Pallas kernels, on_device(): pl.pallas_call(primal_kernel, grid=(BASES,), out_shape=(jax.ShapeDtypeStr...  15.9 us
    unnamed x16, local copies, waits for them, and re-layouts  6.55 us
    pallas_call x1, Pallas kernels, on_device(): pl.pallas_call(dual_kernel, grid=(BASES,), out_shape=(jax.ShapeDtypeStruc...  6.02 us

profile of v1, /device:TPU:0, one launch (start us, length us, event | category | flops | bytes accessed | tf_op | source)
XLA Modules:
  0.0 29.1 jit_solution(9920619095112888476)
XLA Ops:
  0.6 0.0 copy-start
  0.6 2.2 %copy-done = bf16[2,8,512,256]{3,2,1,0:T(8,128)(2,1)S(1)} copy-done((bf16[2,8,512,256]{3,2,1,0:T(8,128)(2,1)S(1)}, bf16[2,8,512,256]{3,2,1,0:T(8,128)(2,1)}, u32[]{:S(2)}) %copy-start) | copy-done | bytes 4194328
  2.8 0.0 copy-start.2
  2.8 1.2 %copy-done.2 = f32[8,7,32,128]{3,2,1,0:T(8,128)S(1)} copy-done((f32[8,7,32,128]{3,2,1,0:T(8,128)S(1)}, f32[8,7,32,128]{3,2,1,0:T(8,128)}, u32[]{:S(2)}) %copy-start.2) | copy-done | bytes 917528
  4.0 0.0 copy-start.3
  4.0 1.7 %copy-done.3 = bf16[2,8,320,224]{3,2,1,0:T(8,128)(2,1)S(1)} copy-done((bf16[2,8,320,224]{3,2,1,0:T(8,128)(2,1)S(1)}, bf16[2,8,320,224]{3,2,1,0:T(8,128)(2,1)}, u32[]{:S(2)}) %copy-start.3) | copy-done | bytes 2293784
  5.7 0.0 copy-start.5
  5.7 0.7 %copy-done.5 = f32[32,128]{1,0:T(8,128)S(1)} copy-done((f32[32,128]{1,0:T(8,128)S(1)}, f32[32,128]{1,0:T(8,128)}, u32[]{:S(2)}) %copy-start.5) | copy-done | bytes 16408
  6.5 0.0 copy-start.6
  6.5 0.7 %copy-done.6 = f32[32,128]{1,0:T(8,128)S(1)} copy-done((f32[32,128]{1,0:T(8,128)S(1)}, f32[32,128]{1,0:T(8,128)}, u32[]{:S(2)}) %copy-start.6) | copy-done | bytes 16408
  7.2 0.0 copy-start.1
  7.2 0.0 copy-start.4
  7.2 0.0 copy-start.7
  7.2 15.9 %shard_map.86 = (bf16[160,256]{1,0:T(8,128)(2,1)S(1)}, f32[32,128]{1,0:T(8,128)S(1)}) custom-call(f32[32,128]{1,0:T(8,128)S(1)} %copy-done.5, f32[32,128]{1,0:T(8,128)S(1)} %copy-done.6, f32[8,224,128]{2,1,0:T(8,128)S(1)} %bitcast.2, bf16[2,8,320,224]{3,2,1,0:T(8,128)(2,1)S(1)} %copy-done.3, bf16[2,8,512,256]{3,2,1,0:T(8,128)(2,1)S(1)} %copy-done), custom_call_target="tpu_custom_call" | custom-call | tf_op jit(solution)/shard_map/pallas_call | solution.py:336
  23.1 0.0 copy-done.1
  23.1 0.0 copy-done.4
  23.1 0.0 copy-done.7
  23.1 6.0 %shard_map.87 = (f32[32,128]{1,0:T(8,128)}, f32[8,224,128]{2,1,0:T(8,128)}) custom-call(f32[8,7]{1,0:T(8,128)S(1)} %copy-done.7, bf16[160,256]{1,0:T(8,128)(2,1)S(1)} %get-tuple-element.6.e_ref, f32[32,128]{1,0:T(8,128)S(1)} %get-tuple-element.7.img_ref, f32[8,224,128]{2,1,0:T(8,128)S(1)} %bitcast.3, bf16[2,8,224,160]{3,2,1,0:T(8,128)(2,1)S(1)} %copy-done.4, ...), custom_call_target="tpu_custom_call" | custom-call | tf_op jit(solution)/shard_map/pallas_call | solution.py:360
Async XLA Ops:
  0.6 2.2 %copy-start = (bf16[2,8,512,256]{3,2,1,0:T(8,128)(2,1)S(1)}, bf16[2,8,512,256]{3,2,1,0:T(8,128)(2,1)}, u32[]{:S(2)}) copy-start(bf16[2,8,512,256]{3,2,1,0:T(8,128)(2,1)} %constant.8.clone.c_ref) | copy-start | bytes 12582916
  2.8 1.2 %copy-start.2 = (f32[8,7,32,128]{3,2,1,0:T(8,128)S(1)}, f32[8,7,32,128]{3,2,1,0:T(8,128)}, u32[]{:S(2)}) copy-start(f32[8,7,32,128]{3,2,1,0:T(8,128)} %param.9) | copy-start | bytes 2752516
  4.0 1.7 %copy-start.3 = (bf16[2,8,320,224]{3,2,1,0:T(8,128)(2,1)S(1)}, bf16[2,8,320,224]{3,2,1,0:T(8,128)(2,1)}, u32[]{:S(2)}) copy-start(bf16[2,8,320,224]{3,2,1,0:T(8,128)(2,1)} %constant.6.clone.a_ref) | copy-start | bytes 6881284
  5.7 0.7 %copy-start.5 = (f32[32,128]{1,0:T(8,128)S(1)}, f32[32,128]{1,0:T(8,128)}, u32[]{:S(2)}) copy-start(f32[32,128]{1,0:T(8,128)} %it_ref.1) | copy-start | bytes 49156
  6.5 0.7 %copy-start.6 = (f32[32,128]{1,0:T(8,128)S(1)}, f32[32,128]{1,0:T(8,128)}, u32[]{:S(2)}) copy-start(f32[32,128]{1,0:T(8,128)} %gr_ref.1) | copy-start | bytes 49156
  7.2 15.9 %copy-start.1 = (bf16[2,8,512,256]{3,2,1,0:T(8,128)(2,1)S(1)}, bf16[2,8,512,256]{3,2,1,0:T(8,128)(2,1)}, u32[]{:S(2)}) copy-start(bf16[2,8,512,256]{3,2,1,0:T(8,128)(2,1)} %constant.8.clone.c_ref) | copy-start | bytes 12582916
  7.2 15.9 %copy-start.4 = (bf16[2,8,224,160]{3,2,1,0:T(8,128)(2,1)S(1)}, bf16[2,8,224,160]{3,2,1,0:T(8,128)(2,1)}, u32[]{:S(2)}) copy-start(bf16[2,8,224,160]{3,2,1,0:T(8,128)(2,1)} %constant.7.clone.b_ref) | copy-start | bytes 3440644
  7.2 15.9 %copy-start.7 = (f32[8,7]{1,0:T(8,128)S(1)}, f32[8,7]{1,0:T(8,128)}, u32[]{:S(2)}) copy-start(f32[8,7]{1,0:T(8,128)} %wt_ref.1) | copy-start | bytes 676

commit v2 on v1

--- a/solution.py
+++ b/solution.py
@@ -13,6 +13,8 @@
 BASES = 8
 BANDS = 7
 REACH = 24
+GROUP = 2
+VMEM_LIMIT = 60 * 2**20
 MESH = pl.DeviceIdType.MESH
 
 primal_step = 0.5
@@ -170,15 +172,15 @@
     return pair[:, :width] + (pair[:, width:] + rest)
 
 
-def synth_one(x, a_ref, c_ref, h, w):
-    span = h + 2 * REACH
-    z = left_dot(a_ref[0, 0], a_ref[1, 0], x)
-    z = jnp.concatenate([z[k * span : (k + 1) * span] for k in range(4)], axis=1)
+def synth_one(x_ref, a_ref, c_ref, k, h, w):
+    span = h + 2 * REACH
+    z = left_dot(a_ref[0, k], a_ref[1, k], x_ref[k])
+    z = jnp.concatenate([z[i * span : (i + 1) * span] for i in range(4)], axis=1)
     high, low = split(z)
     pair = jnp.dot(
-        jnp.concatenate([high, low], axis=0), c_ref[0, 0], preferred_element_type=jnp.float32
+        jnp.concatenate([high, low], axis=0), c_ref[0, k], preferred_element_type=jnp.float32
     )
-    rest = jnp.dot(high, c_ref[1, 0], preferred_element_type=jnp.float32)
+    rest = jnp.dot(high, c_ref[1, k], preferred_element_type=jnp.float32)
     return pair[:span] + (pair[span:] + rest)
 
 
@@ -246,13 +248,19 @@
         held[1, REACH : REACH + h] = it_ref[...]
         acc[...] = jnp.zeros_like(acc)
         acc[REACH : REACH + h, :w] = it_ref[...] - primal_step * gr_ref[...]
-        pl.semaphore_wait(barrier, len(partners()))
+
+    @pl.when(step == 1)
+    def _():
+        pl.semaphore_wait(pltpu.get_barrier_semaphore(), len(partners()))
         for i, (dr, dc) in enumerate(near()):
             held_copy(i, dr, dc).start()
 
-    acc[...] += -primal_step * synth_one(x_ref[0], a_ref, c_ref, h, w)
-
-    @pl.when(step == BASES - 1)
+    total = synth_one(x_ref, a_ref, c_ref, 0, h, w)
+    for k in range(1, GROUP):
+        total = total + synth_one(x_ref, a_ref, c_ref, k, h, w)
+    acc[...] += -primal_step * total
+
+    @pl.when(step == BASES // GROUP - 1)
     def _():
         left = lax.broadcasted_iota(jnp.int32, (span, w), 1) < w // 2
         mine, over = acc[:, :w], acc[:, w:]
@@ -307,22 +315,25 @@
         img_out[...] = img_ref[...]
 
     across = (((1,), (1,)), ((), ()))
-    pair = lax.dot_general(e_ref[...], c_ref[0, 0], across, preferred_element_type=jnp.float32)
-    rest = lax.dot_general(
-        e_ref[:span], c_ref[1, 0], across, preferred_element_type=jnp.float32
-    )
-    z = pair[:span] + (pair[span:] + rest)
-    for first, last, at in ((0, 3, 0), (3, 7, 2)):
-        data = jnp.concatenate(
-            [z[:, at * w : (at + 1) * w], z[:, (at + 1) * w : (at + 2) * w]], axis=0
-        )
-        rows = slice(first * h, last * h)
-        coeffs = left_dot(b_ref[0, 0, rows], b_ref[1, 0, rows], data)
-        for band in range(first, last):
-            bound = wt_ref[step, band]
-            value = x_ref[0, band * h : (band + 1) * h]
-            value = value + coeffs[(band - first) * h : (band - first + 1) * h]
-            x_out[0, band * h : (band + 1) * h] = jnp.clip(value, -bound, bound)
+    for k in range(GROUP):
+        pair = lax.dot_general(
+            e_ref[...], c_ref[0, k], across, preferred_element_type=jnp.float32
+        )
+        rest = lax.dot_general(
+            e_ref[:span], c_ref[1, k], across, preferred_element_type=jnp.float32
+        )
+        z = pair[:span] + (pair[span:] + rest)
+        for first, last, at in ((0, 3, 0), (3, 7, 2)):
+            data = jnp.concatenate(
+                [z[:, at * w : (at + 1) * w], z[:, (at + 1) * w : (at + 2) * w]], axis=0
+            )
+            rows = slice(first * h, last * h)
+            coeffs = left_dot(b_ref[0, k, rows], b_ref[1, k, rows], data)
+            for band in range(first, last):
+                bound = wt_ref[step * GROUP + k, band]
+                value = x_ref[k, band * h : (band + 1) * h]
+                value = value + coeffs[(band - first) * h : (band - first + 1) * h]
+                x_out[k, band * h : (band + 1) * h] = jnp.clip(value, -bound, bound)
 
 
 def on_device(iterate, gradient, dual_coeffs, weights):
@@ -331,11 +342,11 @@
     a, b, c = [jnp.asarray(m) for m in matrices(h, w)]
     duals = dual_coeffs.reshape(BASES, BANDS * h, w)
     whole = pl.BlockSpec((h, w), lambda i: (0, 0))
-    per_basis = pl.BlockSpec((1, BANDS * h, w), lambda i: (i, 0, 0))
-    halved = lambda m: pl.BlockSpec((2, 1) + m.shape[2:], lambda i: (0, i, 0, 0))
+    per_basis = pl.BlockSpec((GROUP, BANDS * h, w), lambda i: (i, 0, 0))
+    halved = lambda m: pl.BlockSpec((2, GROUP) + m.shape[2:], lambda i: (0, i, 0, 0))
     ext, image = pl.pallas_call(
         primal_kernel,
-        grid=(BASES,),
+        grid=(BASES // GROUP,),
         out_shape=(
             jax.ShapeDtypeStruct((2 * span, 2 * w), jnp.bfloat16),
             jax.ShapeDtypeStruct((h, w), jnp.float32),
@@ -354,12 +365,12 @@
             pltpu.SemaphoreType.DMA((14,)),
         ],
         compiler_params=pltpu.CompilerParams(
-            collective_id=0, has_side_effects=True, vmem_limit_bytes=24 * 2**20
+            collective_id=0, has_side_effects=True, vmem_limit_bytes=VMEM_LIMIT
         ),
     )(iterate, gradient, duals, a, c)
     new_image, new_duals = pl.pallas_call(
         dual_kernel,
-        grid=(BASES,),
+        grid=(BASES // GROUP,),
         out_shape=(
             jax.ShapeDtypeStruct((h, w), jnp.float32),
             jax.ShapeDtypeStruct(duals.shape, jnp.float32),
@@ -373,7 +384,7 @@
             halved(c),
         ],
         out_specs=(whole, per_basis),
-        compiler_params=pltpu.CompilerParams(vmem_limit_bytes=24 * 2**20),
+        compiler_params=pltpu.CompilerParams(vmem_limit_bytes=VMEM_LIMIT),
     )(weights, ext, image, duals, b, c)
     return new_image, new_duals.reshape(dual_coeffs.shape)
 

time: 29.5 us -> 23.5 us (0.80)
  local copies, waits for them, and re-layouts: 6.55 us -> 0 us
  Pallas kernels: 21.9 us -> 22.6 us
    unnamed x16 -> x0, local copies, waits for them, and re-layouts: 6.55 us -> none
    pallas_call x2, Pallas kernels: 21.9 us -> 22.6 us  [the longest x1 16.1 us: on_device(): pl.pallas_call(primal_kernel, grid=(BASES // GROUP,), out_shape=(jax.Shap...]
where the time goes in v2:
time: 23.5 us; the launch traced here: 23.3 us
  Pallas kernels  22.6 us (96%)
  between operations  0.64 us (3%)
    pallas_call x1, Pallas kernels, on_device(): pl.pallas_call(primal_kernel, grid=(BASES // GROUP,), out_shape=(jax.Shap...  16.1 us
    pallas_call x1, Pallas kernels, on_device(): pl.pallas_call(dual_kernel, grid=(BASES // GROUP,), out_shape=(jax.ShapeD...  6.55 us

profile of v2, /device:TPU:0, one launch (start us, length us, event | category | flops | bytes accessed | tf_op | source)
XLA Modules:
  0.0 23.3 jit_solution(4743882169012447043)
XLA Ops:
  0.6 16.1 %shard_map.86 = (bf16[160,256]{1,0:T(8,128)(2,1)}, f32[32,128]{1,0:T(8,128)}) custom-call(f32[32,128]{1,0:T(8,128)} %it_ref.1, f32[32,128]{1,0:T(8,128)} %gr_ref.1, f32[8,224,128]{2,1,0:T(8,128)} %bitcast.2, bf16[2,8,320,224]{3,2,1,0:T(8,128)(2,1)} %constant.6.clone.a_ref, bf16[2,8,512,256]{3,2,1,0:T(8,128)(2,1)} %constant.8.clone.c_ref), custom_call_target="tpu_custom_call" | custom-call | tf_op jit(solution)/shard_map/pallas_call | solution.py:347
  16.7 6.5 %shard_map.87 = (f32[32,128]{1,0:T(8,128)}, f32[8,224,128]{2,1,0:T(8,128)}) custom-call(f32[8,7]{1,0:T(8,128)} %wt_ref.1, bf16[160,256]{1,0:T(8,128)(2,1)} %get-tuple-element.6.e_ref, f32[32,128]{1,0:T(8,128)} %get-tuple-element.7.img_ref, f32[8,224,128]{2,1,0:T(8,128)} %bitcast.3, bf16[2,8,224,160]{3,2,1,0:T(8,128)(2,1)} %constant.7.clone.b_ref, ...), custom_call_target="tpu_custom_call" | custom-call | tf_op jit(solution)/shard_map/pallas_call | solution.py:371

commit v3 on v2

--- a/solution.py
+++ b/solution.py
@@ -137,7 +137,7 @@
     scale = 1.0 / math.sqrt(BASES)
     a = np.zeros((BASES, 4 * span, BANDS * h))
     b = np.zeros((BASES, BANDS * h, 2 * span))
-    c = np.zeros((BASES, 4 * w, 2 * w))
+    c = np.zeros((BASES, 8, 2 * w), np.float32)
     kinds = [(1, 0), (0, 1), (1, 1), (3, 2), (2, 3), (3, 3), (2, 2)]
     for basis in range(BASES):
         filters = composite(basis)
@@ -146,20 +146,27 @@
             for off, tap in filters[kind].items():
                 for j in range(h):
                     rows[kind, j, j + REACH + off] += scale * tap
-                for j in range(w):
-                    c[basis, kind * w + j, (j + off) % (2 * w)] += tap
+                c[basis, kind, off % (2 * w)] += tap
         for band, (row_kind, col_kind) in enumerate(kinds):
             mat = rows[row_kind]
             a[basis, col_kind * span : (col_kind + 1) * span, band * h : (band + 1) * h] = mat.T
             at = col_kind % 2
             b[basis, band * h : (band + 1) * h, at * span : (at + 1) * span] = mat
-    return halves(a), halves(b), halves(c)
+    return halves(a), halves(b), c
 
 
 def split(x):
     high = x.astype(jnp.bfloat16)
     low = (x - high.astype(jnp.float32)).astype(jnp.bfloat16)
     return high, low
+
+
+def column_matrix(c_ref, k, w):
+    parts = []
+    for kind in range(4):
+        first = jnp.broadcast_to(c_ref[k, kind : kind + 1], (w, 2 * w))
+        parts.append(pltpu.roll(first, 0, 1, stride=1, stride_axis=0))
+    return split(jnp.concatenate(parts, axis=0))
 
 
 def left_dot(m_high, m_low, x):
@@ -177,10 +184,11 @@
     z = left_dot(a_ref[0, k], a_ref[1, k], x_ref[k])
     z = jnp.concatenate([z[i * span : (i + 1) * span] for i in range(4)], axis=1)
     high, low = split(z)
+    c_high, c_low = column_matrix(c_ref, k, w)
     pair = jnp.dot(
-        jnp.concatenate([high, low], axis=0), c_ref[0, k], preferred_element_type=jnp.float32
+        jnp.concatenate([high, low], axis=0), c_high, preferred_element_type=jnp.float32
     )
-    rest = jnp.dot(high, c_ref[1, k], preferred_element_type=jnp.float32)
+    rest = jnp.dot(high, c_low, preferred_element_type=jnp.float32)
     return pair[:span] + (pair[span:] + rest)
 
 
@@ -316,11 +324,12 @@
 
     across = (((1,), (1,)), ((), ()))
     for k in range(GROUP):
+        c_high, c_low = column_matrix(c_ref, k, w)
         pair = lax.dot_general(
-            e_ref[...], c_ref[0, k], across, preferred_element_type=jnp.float32
+            e_ref[...], c_high, across, preferred_element_type=jnp.float32
         )
         rest = lax.dot_general(
-            e_ref[:span], c_ref[1, k], across, preferred_element_type=jnp.float32
+            e_ref[:span], c_low, across, preferred_element_type=jnp.float32
         )
         z = pair[:span] + (pair[span:] + rest)
         for first, last, at in ((0, 3, 0), (3, 7, 2)):
@@ -343,6 +352,7 @@
     duals = dual_coeffs.reshape(BASES, BANDS * h, w)
     whole = pl.BlockSpec((h, w), lambda i: (0, 0))
     per_basis = pl.BlockSpec((GROUP, BANDS * h, w), lambda i: (i, 0, 0))
+    first_rows = pl.BlockSpec((GROUP, 8, 2 * w), lambda i: (i, 0, 0))
     halved = lambda m: pl.BlockSpec((2, GROUP) + m.shape[2:], lambda i: (0, i, 0, 0))
     ext, image = pl.pallas_call(
         primal_kernel,
@@ -351,7 +361,7 @@
             jax.ShapeDtypeStruct((2 * span, 2 * w), jnp.bfloat16),
             jax.ShapeDtypeStruct((h, w), jnp.float32),
         ),
-        in_specs=[whole, whole, per_basis, halved(a), halved(c)],
+        in_specs=[whole, whole, per_basis, halved(a), first_rows],
         out_specs=(pl.BlockSpec((2 * span, 2 * w), lambda i: (0, 0)), whole),
         scratch_shapes=[
             pltpu.VMEM((span, 2 * w), jnp.float32),
@@ -381,7 +391,7 @@
             whole,
             per_basis,
             halved(b),
-            halved(c),
+            first_rows,
         ],
         out_specs=(whole, per_basis),
         compiler_params=pltpu.CompilerParams(vmem_limit_bytes=VMEM_LIMIT),

time: 23.5 us -> 22.6 us (0.962)
  Pallas kernels: 22.6 us -> 21.7 us
    pallas_call x1, Pallas kernels: 16.1 us -> 15.6 us  [on_device(): pl.pallas_call(primal_kernel, grid=(BASES // GROUP,), out_shape=(jax.Shap...]
    pallas_call x1, Pallas kernels: 6.55 us -> 6.09 us  [on_device(): pl.pallas_call(dual_kernel, grid=(BASES // GROUP,), out_shape=(jax.ShapeD...]
where the time goes in v3:
time: 22.6 us; the launch traced here: 22.4 us
  Pallas kernels  21.7 us (96%)
  between operations  0.64 us (3%)
    pallas_call x1, Pallas kernels, on_device(): pl.pallas_call(primal_kernel, grid=(BASES // GROUP,), out_shape=(jax.Shap...  15.6 us
    pallas_call x1, Pallas kernels, on_device(): pl.pallas_call(dual_kernel, grid=(BASES // GROUP,), out_shape=(jax.ShapeD...  6.09 us

profile of v3, /device:TPU:0, one launch (start us, length us, event | category | flops | bytes accessed | tf_op | source)
XLA Modules:
  0.0 22.4 jit_solution(6172422774202612394)
XLA Ops:
  0.6 15.6 %shard_map.86 = (bf16[160,256]{1,0:T(8,128)(2,1)}, f32[32,128]{1,0:T(8,128)}) custom-call(f32[32,128]{1,0:T(8,128)} %it_ref.1, f32[32,128]{1,0:T(8,128)} %gr_ref.1, f32[8,224,128]{2,1,0:T(8,128)} %bitcast.2, bf16[2,8,320,224]{3,2,1,0:T(8,128)(2,1)} %constant.6.clone.a_ref, f32[8,8,256]{2,1,0:T(8,128)} %constant.8.clone.c_ref), custom_call_target="tpu_custom_call" | custom-call | tf_op jit(solution)/shard_map/pallas_call | solution.py:357
  16.3 6.1 %shard_map.87 = (f32[32,128]{1,0:T(8,128)}, f32[8,224,128]{2,1,0:T(8,128)}) custom-call(f32[8,7]{1,0:T(8,128)} %wt_ref.1, bf16[160,256]{1,0:T(8,128)(2,1)} %get-tuple-element.6.e_ref, f32[32,128]{1,0:T(8,128)} %get-tuple-element.7.img_ref, f32[8,224,128]{2,1,0:T(8,128)} %bitcast.3, bf16[2,8,224,160]{3,2,1,0:T(8,128)(2,1)} %constant.7.clone.b_ref, ...), custom_call_target="tpu_custom_call" | custom-call | tf_op jit(solution)/shard_map/pallas_call | solution.py:381

commit v4 on v3

--- a/solution.py
+++ b/solution.py
@@ -13,7 +13,7 @@
 BASES = 8
 BANDS = 7
 REACH = 24
-GROUP = 2
+GROUP = 4
 VMEM_LIMIT = 60 * 2**20
 MESH = pl.DeviceIdType.MESH
 

time: 22.6 us -> 21.4 us (0.947)
  Pallas kernels: 21.7 us -> 20.7 us
    pallas_call x1, Pallas kernels: 15.6 us -> 15.1 us  [on_device(): pl.pallas_call(primal_kernel, grid=(BASES // GROUP,), out_shape=(jax.Shap...]
    pallas_call x1, Pallas kernels: 6.09 us -> 5.57 us  [on_device(): pl.pallas_call(dual_kernel, grid=(BASES // GROUP,), out_shape=(jax.ShapeD...]
where the time goes in v4:
time: 21.4 us; the launch traced here: 21.3 us
  Pallas kernels  20.7 us (97%)
  between operations  0.64 us (3%)
    pallas_call x1, Pallas kernels, on_device(): pl.pallas_call(primal_kernel, grid=(BASES // GROUP,), out_shape=(jax.Shap...  15.1 us
    pallas_call x1, Pallas kernels, on_device(): pl.pallas_call(dual_kernel, grid=(BASES // GROUP,), out_shape=(jax.ShapeD...  5.57 us

profile of v4, /device:TPU:0, one launch (start us, length us, event | category | flops | bytes accessed | tf_op | source)
XLA Modules:
  0.0 21.3 jit_solution(7927853956224752852)
XLA Ops:
  0.6 15.1 %shard_map.86 = (bf16[160,256]{1,0:T(8,128)(2,1)}, f32[32,128]{1,0:T(8,128)}) custom-call(f32[32,128]{1,0:T(8,128)} %it_ref.1, f32[32,128]{1,0:T(8,128)} %gr_ref.1, f32[8,224,128]{2,1,0:T(8,128)} %bitcast.2, bf16[2,8,320,224]{3,2,1,0:T(8,128)(2,1)} %constant.6.clone.a_ref, f32[8,8,256]{2,1,0:T(8,128)} %constant.8.clone.c_ref), custom_call_target="tpu_custom_call" | custom-call | tf_op jit(solution)/shard_map/pallas_call | solution.py:357
  15.7 5.6 %shard_map.87 = (f32[32,128]{1,0:T(8,128)}, f32[8,224,128]{2,1,0:T(8,128)}) custom-call(f32[8,7]{1,0:T(8,128)} %wt_ref.1, bf16[160,256]{1,0:T(8,128)(2,1)} %get-tuple-element.6.e_ref, f32[32,128]{1,0:T(8,128)} %get-tuple-element.7.img_ref, f32[8,224,128]{2,1,0:T(8,128)} %bitcast.3, bf16[2,8,224,160]{3,2,1,0:T(8,128)(2,1)} %constant.7.clone.b_ref, ...), custom_call_target="tpu_custom_call" | custom-call | tf_op jit(solution)/shard_map/pallas_call | solution.py:381

commit v5 on v4

--- a/solution.py
+++ b/solution.py
@@ -15,6 +15,8 @@
 REACH = 24
 GROUP = 4
 VMEM_LIMIT = 60 * 2**20
+COLUMN_BANDS = [(0,), (1, 2), (3, 6), (4, 5)]
+BAND_ORDER = [0, 1, 2, 3, 6, 4, 5]
 MESH = pl.DeviceIdType.MESH
 
 primal_step = 0.5
@@ -135,8 +137,8 @@
 def matrices(h, w):
     span = h + 2 * REACH
     scale = 1.0 / math.sqrt(BASES)
-    a = np.zeros((BASES, 4 * span, BANDS * h))
-    b = np.zeros((BASES, BANDS * h, 2 * span))
+    a = np.zeros((BASES, 4 * span, 2 * h))
+    b = np.zeros((BASES, BANDS * h, span))
     c = np.zeros((BASES, 8, 2 * w), np.float32)
     kinds = [(1, 0), (0, 1), (1, 1), (3, 2), (2, 3), (3, 3), (2, 2)]
     for basis in range(BASES):
@@ -149,9 +151,10 @@
                 c[basis, kind, off % (2 * w)] += tap
         for band, (row_kind, col_kind) in enumerate(kinds):
             mat = rows[row_kind]
-            a[basis, col_kind * span : (col_kind + 1) * span, band * h : (band + 1) * h] = mat.T
-            at = col_kind % 2
-            b[basis, band * h : (band + 1) * h, at * span : (at + 1) * span] = mat
+            at = COLUMN_BANDS[col_kind].index(band)
+            a[basis, col_kind * span : (col_kind + 1) * span, at * h : (at + 1) * h] = mat.T
+            place = BAND_ORDER.index(band)
+            b[basis, place * h : (place + 1) * h] = mat
     return halves(a), halves(b), c
 
 
@@ -181,8 +184,13 @@
 
 def synth_one(x_ref, a_ref, c_ref, k, h, w):
     span = h + 2 * REACH
-    z = left_dot(a_ref[0, k], a_ref[1, k], x_ref[k])
-    z = jnp.concatenate([z[i * span : (i + 1) * span] for i in range(4)], axis=1)
+    parts = []
+    for kind, bands in enumerate(COLUMN_BANDS):
+        rows, depth = slice(kind * span, (kind + 1) * span), len(bands) * h
+        data = [x_ref[k, band * h : (band + 1) * h] for band in bands]
+        data = jnp.concatenate(data, axis=0) if len(data) > 1 else data[0]
+        parts.append(left_dot(a_ref[0, k, rows, :depth], a_ref[1, k, rows, :depth], data))
+    z = jnp.concatenate(parts, axis=1)
     high, low = split(z)
     c_high, c_low = column_matrix(c_ref, k, w)
     pair = jnp.dot(
@@ -332,16 +340,15 @@
             e_ref[:span], c_low, across, preferred_element_type=jnp.float32
         )
         z = pair[:span] + (pair[span:] + rest)
-        for first, last, at in ((0, 3, 0), (3, 7, 2)):
-            data = jnp.concatenate(
-                [z[:, at * w : (at + 1) * w], z[:, (at + 1) * w : (at + 2) * w]], axis=0
-            )
-            rows = slice(first * h, last * h)
+        done = 0
+        for kind, bands in enumerate(COLUMN_BANDS):
+            rows = slice(done * h, (done + len(bands)) * h)
+            done += len(bands)
+            data = z[:, kind * w : (kind + 1) * w]
             coeffs = left_dot(b_ref[0, k, rows], b_ref[1, k, rows], data)
-            for band in range(first, last):
+            for at, band in enumerate(bands):
                 bound = wt_ref[step * GROUP + k, band]
-                value = x_ref[k, band * h : (band + 1) * h]
-                value = value + coeffs[(band - first) * h : (band - first + 1) * h]
+                value = x_ref[k, band * h : (band + 1) * h] + coeffs[at * h : (at + 1) * h]
                 x_out[k, band * h : (band + 1) * h] = jnp.clip(value, -bound, bound)
 
 

time: 21.4 us -> 21.1 us (0.986)
  Pallas kernels: 20.7 us -> 20.3 us
where the time goes in v5:
time: 21.1 us; the launch traced here: 20.9 us
  Pallas kernels  20.3 us (96%)
  between operations  0.64 us (3%)
    pallas_call x1, Pallas kernels, on_device(): pl.pallas_call(primal_kernel, grid=(BASES // GROUP,), out_shape=(jax.Shap...  14.9 us
    pallas_call x1, Pallas kernels, on_device(): pl.pallas_call(dual_kernel, grid=(BASES // GROUP,), out_shape=(jax.ShapeD...  5.36 us

profile of v5, /device:TPU:0, one launch (start us, length us, event | category | flops | bytes accessed | tf_op | source)
XLA Modules:
  0.0 20.9 jit_solution(8123471485010832546)
XLA Ops:
  0.6 14.9 %shard_map.86 = (bf16[160,256]{1,0:T(8,128)(2,1)}, f32[32,128]{1,0:T(8,128)}) custom-call(f32[32,128]{1,0:T(8,128)} %it_ref.1, f32[32,128]{1,0:T(8,128)} %gr_ref.1, f32[8,224,128]{2,1,0:T(8,128)} %bitcast.2, bf16[2,8,320,64]{3,2,1,0:T(8,128)(2,1)} %constant.6.clone.a_ref, f32[8,8,256]{2,1,0:T(8,128)} %constant.8.clone.c_ref), custom_call_target="tpu_custom_call" | custom-call | tf_op jit(solution)/shard_map/pallas_call | solution.py:364
  15.6 5.4 %shard_map.87 = (f32[32,128]{1,0:T(8,128)}, f32[8,224,128]{2,1,0:T(8,128)}) custom-call(f32[8,7]{1,0:T(8,128)} %wt_ref.1, bf16[160,256]{1,0:T(8,128)(2,1)} %get-tuple-element.6.e_ref, f32[32,128]{1,0:T(8,128)} %get-tuple-element.7.img_ref, f32[8,224,128]{2,1,0:T(8,128)} %bitcast.3, bf16[2,8,224,80]{3,2,1,0:T(8,128)(2,1)} %constant.7.clone.b_ref, ...), custom_call_target="tpu_custom_call" | custom-call | tf_op jit(solution)/shard_map/pallas_call | solution.py:388

commit v6 on v5

--- a/solution.py
+++ b/solution.py
@@ -14,7 +14,7 @@
 BANDS = 7
 REACH = 24
 GROUP = 4
-VMEM_LIMIT = 60 * 2**20
+VMEM_LIMIT = 24 * 2**20
 COLUMN_BANDS = [(0,), (1, 2), (3, 6), (4, 5)]
 BAND_ORDER = [0, 1, 2, 3, 6, 4, 5]
 MESH = pl.DeviceIdType.MESH

time: 21.1 us -> 23.8 us (1.13)
  local copies, waits for them, and re-layouts: 0 us -> 4.77 us
  Pallas kernels: 20.3 us -> 18 us
    unnamed x0 -> x16, local copies, waits for them, and re-layouts: none -> 4.77 us
    pallas_call x1, Pallas kernels: 14.9 us -> 13.2 us  [on_device(): pl.pallas_call(primal_kernel, grid=(BASES // GROUP,), out_shape=(jax.Shap...]
    pallas_call x1, Pallas kernels: 5.36 us -> 4.8 us  [on_device(): pl.pallas_call(dual_kernel, grid=(BASES // GROUP,), out_shape=(jax.ShapeD...]
where the time goes in v6:
time: 23.8 us; the launch traced here: 23.5 us
  Pallas kernels  18 us (76%)
  local copies, waits for them, and re-layouts  4.77 us (20%)
  between operations  0.68 us (3%)
    pallas_call x1, Pallas kernels, on_device(): pl.pallas_call(primal_kernel, grid=(BASES // GROUP,), out_shape=(jax.Shap...  13.2 us
    pallas_call x1, Pallas kernels, on_device(): pl.pallas_call(dual_kernel, grid=(BASES // GROUP,), out_shape=(jax.ShapeD...  4.8 us
    unnamed x16, local copies, waits for them, and re-layouts  4.77 us

profile of v6, /device:TPU:0, one launch (start us, length us, event | category | flops | bytes accessed | tf_op | source)
XLA Modules:
  0.0 23.5 jit_solution(14765196342913694254)
XLA Ops:
  0.6 0.0 copy-start
  0.6 1.2 %copy-done = f32[8,7,32,128]{3,2,1,0:T(8,128)S(1)} copy-done((f32[8,7,32,128]{3,2,1,0:T(8,128)S(1)}, f32[8,7,32,128]{3,2,1,0:T(8,128)}, u32[]{:S(2)}) %copy-start) | copy-done | bytes 917528
  1.8 0.0 copy-start.2
  1.8 1.3 %copy-done.2 = bf16[2,8,320,64]{3,2,1,0:T(8,128)(2,1)S(1)} copy-done((bf16[2,8,320,64]{3,2,1,0:T(8,128)(2,1)S(1)}, bf16[2,8,320,64]{3,2,1,0:T(8,128)(2,1)}, u32[]{:S(2)}) %copy-start.2) | copy-done | bytes 655384
  3.1 0.0 copy-start.4
  3.1 0.8 %copy-done.4 = f32[8,8,256]{2,1,0:T(8,128)S(1)} copy-done((f32[8,8,256]{2,1,0:T(8,128)S(1)}, f32[8,8,256]{2,1,0:T(8,128)}, u32[]{:S(2)}) %copy-start.4) | copy-done | bytes 65560
  4.0 0.0 copy-start.5
  4.0 0.7 %copy-done.5 = f32[32,128]{1,0:T(8,128)S(1)} copy-done((f32[32,128]{1,0:T(8,128)S(1)}, f32[32,128]{1,0:T(8,128)}, u32[]{:S(2)}) %copy-start.5) | copy-done | bytes 16408
  4.7 0.0 copy-start.6
  4.7 0.7 %copy-done.6 = f32[32,128]{1,0:T(8,128)S(1)} copy-done((f32[32,128]{1,0:T(8,128)S(1)}, f32[32,128]{1,0:T(8,128)}, u32[]{:S(2)}) %copy-start.6) | copy-done | bytes 16408
  5.4 0.0 copy-start.1
  5.4 0.0 copy-start.3
  5.4 0.0 copy-start.7
  5.4 13.2 %shard_map.86 = (bf16[160,256]{1,0:T(8,128)(2,1)S(1)}, f32[32,128]{1,0:T(8,128)S(1)}) custom-call(f32[32,128]{1,0:T(8,128)S(1)} %copy-done.5, f32[32,128]{1,0:T(8,128)S(1)} %copy-done.6, f32[8,224,128]{2,1,0:T(8,128)S(1)} %bitcast.2, bf16[2,8,320,64]{3,2,1,0:T(8,128)(2,1)S(1)} %copy-done.2, f32[8,8,256]{2,1,0:T(8,128)S(1)} %copy-done.4), custom_call_target="tpu_custom_call" | custom-call | tf_op jit(solution)/shard_map/pallas_call | solution.py:364
  18.6 0.0 copy-done.1
  18.6 0.0 copy-done.3
  18.7 0.0 copy-done.7
  18.7 4.8 %shard_map.87 = (f32[32,128]{1,0:T(8,128)}, f32[8,224,128]{2,1,0:T(8,128)}) custom-call(f32[8,7]{1,0:T(8,128)S(1)} %copy-done.7, bf16[160,256]{1,0:T(8,128)(2,1)S(1)} %get-tuple-element.6.e_ref, f32[32,128]{1,0:T(8,128)S(1)} %get-tuple-element.7.img_ref, f32[8,224,128]{2,1,0:T(8,128)S(1)} %bitcast.3, bf16[2,8,224,80]{3,2,1,0:T(8,128)(2,1)S(1)} %copy-done.3, ...), custom_call_target="tpu_custom_call" | custom-call | tf_op jit(solution)/shard_map/pallas_call | solution.py:388
Async XLA Ops:
  0.6 1.2 %copy-start = (f32[8,7,32,128]{3,2,1,0:T(8,128)S(1)}, f32[8,7,32,128]{3,2,1,0:T(8,128)}, u32[]{:S(2)}) copy-start(f32[8,7,32,128]{3,2,1,0:T(8,128)} %param.9) | copy-start | bytes 2752516
  1.8 1.3 %copy-start.2 = (bf16[2,8,320,64]{3,2,1,0:T(8,128)(2,1)S(1)}, bf16[2,8,320,64]{3,2,1,0:T(8,128)(2,1)}, u32[]{:S(2)}) copy-start(bf16[2,8,320,64]{3,2,1,0:T(8,128)(2,1)} %constant.6.clone.a_ref) | copy-start | bytes 1966084
  3.1 0.8 %copy-start.4 = (f32[8,8,256]{2,1,0:T(8,128)S(1)}, f32[8,8,256]{2,1,0:T(8,128)}, u32[]{:S(2)}) copy-start(f32[8,8,256]{2,1,0:T(8,128)} %constant.8.clone.c_ref) | copy-start | bytes 196612
  4.0 0.7 %copy-start.5 = (f32[32,128]{1,0:T(8,128)S(1)}, f32[32,128]{1,0:T(8,128)}, u32[]{:S(2)}) copy-start(f32[32,128]{1,0:T(8,128)} %it_ref.1) | copy-start | bytes 49156
  4.7 0.7 %copy-start.6 = (f32[32,128]{1,0:T(8,128)S(1)}, f32[32,128]{1,0:T(8,128)}, u32[]{:S(2)}) copy-start(f32[32,128]{1,0:T(8,128)} %gr_ref.1) | copy-start | bytes 49156
  5.4 13.2 %copy-start.1 = (f32[8,7,32,128]{3,2,1,0:T(8,128)S(1)}, f32[8,7,32,128]{3,2,1,0:T(8,128)}, u32[]{:S(2)}) copy-start(f32[8,7,32,128]{3,2,1,0:T(8,128)} %param.9) | copy-start | bytes 2752516
  5.4 13.2 %copy-start.3 = (bf16[2,8,224,80]{3,2,1,0:T(8,128)(2,1)S(1)}, bf16[2,8,224,80]{3,2,1,0:T(8,128)(2,1)}, u32[]{:S(2)}) copy-start(bf16[2,8,224,80]{3,2,1,0:T(8,128)(2,1)} %constant.7.clone.b_ref) | copy-start | bytes 1720324
  5.4 13.3 %copy-start.7 = (f32[8,7]{1,0:T(8,128)S(1)}, f32[8,7]{1,0:T(8,128)}, u32[]{:S(2)}) copy-start(f32[8,7]{1,0:T(8,128)} %wt_ref.1) | copy-start | bytes 676

commit v7 on v6

--- a/solution.py
+++ b/solution.py
@@ -384,7 +384,7 @@
         compiler_params=pltpu.CompilerParams(
             collective_id=0, has_side_effects=True, vmem_limit_bytes=VMEM_LIMIT
         ),
-    )(iterate, gradient, duals, a, c)
+    )(*[pltpu.with_memory_space_constraint(x, pltpu.HBM) for x in (iterate, gradient, duals, a, c)])
     new_image, new_duals = pl.pallas_call(
         dual_kernel,
         grid=(BASES // GROUP,),

time: 23.8 us -> 20.2 us (0.85)
  local copies, waits for them, and re-layouts: 4.77 us -> 0.02 us
  Pallas kernels: 18 us -> 19.4 us
    unnamed x16 -> x8, local copies, waits for them, and re-layouts: 4.77 us -> 0.02 us
    pallas_call x1, Pallas kernels: 13.2 us -> 14.5 us  [on_device(): pl.pallas_call(primal_kernel, grid=(BASES // GROUP,), out_shape=(jax.Shap...]
where the time goes in v7:
time: 20.2 us; the launch traced here: 20.1 us
  Pallas kernels  19.4 us (96%)
  between operations  0.7 us (3%)
    pallas_call x1, Pallas kernels, on_device(): pl.pallas_call(primal_kernel, grid=(BASES // GROUP,), out_shape=(jax.Shap...  14.5 us
    pallas_call x1, Pallas kernels, on_device(): pl.pallas_call(dual_kernel, grid=(BASES // GROUP,), out_shape=(jax.ShapeD...  4.82 us

profile of v7, /device:TPU:0, one launch (start us, length us, event | category | flops | bytes accessed | tf_op | source)
XLA Modules:
  0.0 20.1 jit_solution(10814335231845090008)
XLA Ops:
  0.6 0.0 copy-start.2
  0.6 0.0 copy-start.1
  0.7 0.0 copy-start.3
  0.7 0.0 copy-start
  0.7 14.5 %shard_map.86 = (bf16[160,256]{1,0:T(8,128)(2,1)S(1)}, f32[32,128]{1,0:T(8,128)S(1)}) custom-call(f32[32,128]{1,0:T(8,128)} %it_ref.1, f32[32,128]{1,0:T(8,128)} %gr_ref.1, f32[8,224,128]{2,1,0:T(8,128)} %bitcast.2, bf16[2,8,320,64]{3,2,1,0:T(8,128)(2,1)} %constant.6.clone.a_ref, f32[8,8,256]{2,1,0:T(8,128)} %constant.8.clone.c_ref), custom_call_target="tpu_custom_call" | custom-call | tf_op jit(solution)/shard_map/pallas_call | solution.py:364
  15.2 0.0 copy-done.2
  15.2 0.0 copy-done.1
  15.2 0.0 copy-done.3
  15.3 0.0 copy-done
  15.3 4.8 %shard_map.87 = (f32[32,128]{1,0:T(8,128)}, f32[8,224,128]{2,1,0:T(8,128)}) custom-call(f32[8,7]{1,0:T(8,128)S(1)} %copy-done.3, bf16[160,256]{1,0:T(8,128)(2,1)S(1)} %get-tuple-element.6.e_ref, f32[32,128]{1,0:T(8,128)S(1)} %get-tuple-element.7.img_ref, f32[8,224,128]{2,1,0:T(8,128)S(1)} %bitcast.3, bf16[2,8,224,80]{3,2,1,0:T(8,128)(2,1)S(1)} %copy-done.1, ...), custom_call_target="tpu_custom_call" | custom-call | tf_op jit(solution)/shard_map/pallas_call | solution.py:388
Async XLA Ops:
  0.6 14.6 %copy-start.2 = (f32[8,8,256]{2,1,0:T(8,128)S(1)}, f32[8,8,256]{2,1,0:T(8,128)}, u32[]{:S(2)}) copy-start(f32[8,8,256]{2,1,0:T(8,128)} %constant.8.clone.c_ref) | copy-start | bytes 196612
  0.6 14.6 %copy-start.1 = (bf16[2,8,224,80]{3,2,1,0:T(8,128)(2,1)S(1)}, bf16[2,8,224,80]{3,2,1,0:T(8,128)(2,1)}, u32[]{:S(2)}) copy-start(bf16[2,8,224,80]{3,2,1,0:T(8,128)(2,1)} %constant.7.clone.b_ref) | copy-start | bytes 1720324
  0.7 14.6 %copy-start.3 = (f32[8,7]{1,0:T(8,128)S(1)}, f32[8,7]{1,0:T(8,128)}, u32[]{:S(2)}) copy-start(f32[8,7]{1,0:T(8,128)} %wt_ref.1) | copy-start | bytes 676
  0.7 14.6 %copy-start = (f32[8,7,32,128]{3,2,1,0:T(8,128)S(1)}, f32[8,7,32,128]{3,2,1,0:T(8,128)}, u32[]{:S(2)}) copy-start(f32[8,7,32,128]{3,2,1,0:T(8,128)} %param.9) | copy-start | bytes 2752516
